TPU v7x, 32 devices: a whole 2x2x4 slice. The times are simulated.
32 devices in a mesh: parts: 2 (over y), row: 4 (over z), col: 4 (over x, core).
Axes of the slice: x: 2, y: 2, z: 4, core: 2. Of those that a mesh axis runs over, the one named last changes fastest.
Arguments:
- wavefunction: bfloat16 [128, 128, 128], P('parts', 'col'), parts along dimension 0, may hold values from -6 to 6
- left_ops: bfloat16 [768, 128, 128], P(('parts', 'row')), parts along dimension 0, may hold values from -0.5 to 0.5
- right_ops: bfloat16 [768, 128, 128], P(('parts', 'row'), 'col'), parts along dimension 0, may hold values from -0.0625 to 0.0625
- term_source: int32 [768], P(('parts', 'row')), parts along dimension 0, may hold values from 0 to 63
- term_target: int32 [768], P(('parts', 'row')), parts along dimension 0, may hold values from 0 to 63
- term_count: int32 [8], P(('parts', 'row')), parts along dimension 0, may hold values from 1 to 96, 240 in all
- left_dims: int32 [128], P('parts'), parts along dimension 0, may hold values from 1 to 128, 6144 in all
- right_dims: int32 [128], P('parts'), parts along dimension 0, may hold values from 1 to 128, 5120 in all
Outputs:
- sigmas: float32 [3, 128, 128, 128], P(None, ('parts', 'row'), 'col'), parts along dimension 1
There are 2 independent parts, one for each index of `parts`. A program takes and returns all parts, laid end to end along the dimension named above; each array names one. Nothing has to cross between parts.
Inputs may be any that keep to these rules, and one draw needn't show every extreme that they name: The busiest index of row has exactly 96 live slots; slots from term_count on are unused. `left_dims`: the largest equals 128. `right_dims`: the largest equals 128.
All inputs are finite; a program needn't handle non-finite values. No bound on the sum of `term_count` on one device may be relied on, other than what follows from the above.
Results may differ from a plain program's by a relative error of at most 0.0032.
Values may be sent and summed in bfloat16 or wider, within the bound.
A program may use at most 64 MiB of HBM per device.

v0:
```python
import jax
import jax.numpy as jnp
from jax import lax
from jax.sharding import PartitionSpec as P

group_size = 8


def body(
    wavefunction, left_ops, right_ops, term_source, term_target, term_count, left_dims, right_dims
):
    row_total = lax.axis_size("row")
    col_total = lax.axis_size("col")
    sectors, own_cols, left_size = wavefunction.shape
    per_row = sectors // row_total
    row_place = lax.axis_index("row")
    col_place = lax.axis_index("col")
    term_total = term_count[0]
    cell_total = sectors * own_cols * col_total * left_size
    col_ids = col_place * own_cols + jnp.arange(own_cols, dtype=jnp.int32)
    support_full = (
        (col_ids[None, :, None] < right_dims[:, None, None])
        & (jnp.arange(left_size, dtype=jnp.int32)[None, None, :] < left_dims[:, None, None])
    ).astype(jnp.float32)
    support_own = lax.dynamic_slice_in_dim(support_full, row_place * per_row, per_row, 0)

    def global_sums(values):
        return lax.psum(values, ("row", "col"))

    vector_full = (wavefunction.astype(jnp.float32) * support_full).astype(jnp.bfloat16)
    own_vectors = [lax.dynamic_slice_in_dim(vector_full, row_place * per_row, per_row, 0)]
    norm_list = []
    results = []
    for step in range(3):
        start_sum = jnp.zeros((sectors, own_cols, left_size), jnp.float32)
        column_part = lax.all_gather(vector_full, "col", axis=1, tiled=True)

        def add_group(block_index, accum):
            offset = block_index * group_size
            sources = lax.dynamic_slice_in_dim(term_source, offset, group_size, 0)
            targets = lax.dynamic_slice_in_dim(term_target, offset, group_size, 0)
            weights = (offset + jnp.arange(group_size, dtype=jnp.int32) < term_total).astype(
                jnp.float32
            )
            left_group = lax.dynamic_slice_in_dim(left_ops, offset, group_size, 0)
            right_group = lax.dynamic_slice_in_dim(right_ops, offset, group_size, 0)
            blocks = column_part[sources]
            inner_part = jnp.einsum(
                "gkb,gbc->gkc", blocks, left_group, preferred_element_type=jnp.float32
            )
            term_out = jnp.einsum(
                "gwk,gkc->gwc",
                right_group.astype(jnp.float32),
                inner_part,
                precision=lax.Precision.HIGHEST,
            )
            return accum.at[targets].add(term_out * weights[:, None, None])

        rounds = (term_total + group_size - 1) // group_size
        partial_value = lax.fori_loop(0, rounds, add_group, start_sum)
        summed = lax.psum_scatter(partial_value, "row", scatter_dimension=0, tiled=True)
        sigma = summed * support_own
        results.append(sigma)
        if step + 1 < 3:
            wide = [entry.astype(jnp.float32) for entry in own_vectors]
            correlations, latest_norm = global_sums(
                (
                    jnp.stack([jnp.sum(entry * sigma) for entry in wide]),
                    jnp.sum(wide[-1] * wide[-1]),
                )
            )
            norm_list.append(latest_norm)
            remainder = sigma
            for index in range(step + 1):
                remainder = (
                    remainder - correlations[index] / (norm_list[index] + 1e-06) * wide[index]
                )
            square_sum = global_sums(jnp.sum(remainder * remainder))
            mean_sq = square_sum / cell_total
            next_own = (remainder * lax.rsqrt(mean_sq + 1e-06)).astype(jnp.bfloat16)
            own_vectors.append(next_own)
            vector_full = lax.all_gather(next_own, "row", axis=0, tiled=True)
    return jnp.stack(results)


def solution(mesh):
    placed = (
        P("parts", "col", None),
        P(("parts", "row"), None, None),
        P(("parts", "row"), "col", None),
        P(("parts", "row")),
        P(("parts", "row")),
        P(("parts", "row")),
        P("parts"),
        P("parts"),
    )
    return jax.shard_map(
        body,
        mesh=mesh,
        in_specs=placed,
        out_specs=P(None, ("parts", "row"), "col", None),
        check_vma=False,
    )
```

profile of v0, /device:TPU:0, one launch (start us, length us, event | category | flops | bytes accessed | tf_op | source)
XLA Modules:
  0.0 569.9 jit_solution(13888451957683459120)
XLA Ops:
  8.0 2.2 select_convert_fusion
  10.9 24.7 %all-gather.4.cloned.1.call-done = bf16[64,128,128]{2,1,0:T(8,128)(2,1)} async-done(((bf16[64,32,128]{2,1,0:T(8,128)(2,1)}), bf16[64,128,128]{2,1,0:T(8,128)(2,1)}) %all-gather.4.cloned.1.call-update) | async-done | bytes 2097168 | tf_op jit(solution)/shard_map/all_gather | solution.py:36
  35.8 68.6 %while.30 = (s32[]{:T(128)}, f32[64,32,128]{2,1,0:T(8,128)S(1)}, s32[]{:T(128)}, s32[96]{0:T(128)}, bf16[96,32,128]{2,1,0:T(8,128)(2,1)}, /*index=5*/s32[96]{0:T...) while((s32[]{:T(128)}, f32[64,32,128]{2,1,0:T(8,128)S(1)}, ...), condition=%wide.region_2.3_spmd, body=%wide.region_0.2_spmd.sunk | while | flops 83952720 | bytes 2691551 | solution.py:60
  36.6 2.2 gather_fusion
  43.5 2.2 gather_fusion
  50.3 2.2 gather_fusion
  57.2 2.2 gather_fusion
  64.0 2.2 gather_fusion
  70.9 2.2 gather_fusion
  77.8 2.2 gather_fusion
  84.6 2.2 gather_fusion
  91.5 2.2 gather_fusion
  98.3 2.2 gather_fusion
  105.8 39.7 %reduce-scatter.4.cloned.1.call-done = f32[16,32,128]{2,1,0:T(8,128)} async-done(((f32[64,32,128]{2,1,0:T(8,128)}), f32[16,32,128]{2,1,0:T(8,128)}) %reduce-scatter.4.cloned.1.call-update) | async-done | bytes 262160 | tf_op jit(solution)/shard_map/reduce_scatter | solution.py:61
  145.5 1.7 fusion.20
  147.2 31.1 %all-reduce.1 = (f32[]{:T(128)}, f32[]{:T(128)}) all-reduce(f32[]{:T(128)} %get-tuple-element.155, f32[]{:T(128)} %get-tuple-element.154), channel_id=1, replica_groups=mesh['parts'=2,'row'=4,'col'=4] {'row','col'}, use_global_device_ids=true, to_apply=%region_5.6 | all-reduce | flops 2 | bytes 16 | tf_op jit(solution)/shard_map/psum | solution.py:28
  181.2 30.1 %psum.44 = f32[]{:T(128)} all-reduce(f32[]{:T(128)} %multiply_reduce_fusion.1), channel_id=1, replica_groups=mesh['parts'=2,'row'=4,'col'=4] {'row','col'}, use_global_device_ids=true, to_apply=%region_9.10 | all-reduce | flops 1 | bytes 8 | tf_op jit(solution)/shard_map/psum | solution.py:28
  213.0 17.0 %all_gather.16 = bf16[64,32,128]{2,1,0:T(8,128)(2,1)} all-gather(bf16[16,32,128]{2,1,0:T(8,128)(2,1)S(1)} %multiply_convert_fusion.1), channel_id=1, replica_groups=mesh['parts'=2,'row'=4,'col'=4] {'row'}, dimensions={0}, use_global_device_ids=true | all-gather | bytes 655360 | tf_op jit(solution)/shard_map/all_gather | solution.py:82
  230.1 20.1 %all-gather.6.cloned.1.call-done = bf16[64,128,128]{2,1,0:T(8,128)(2,1)} async-done(((bf16[64,32,128]{2,1,0:T(8,128)(2,1)}), bf16[64,128,128]{2,1,0:T(8,128)(2,1)}) %all-gather.6.cloned.1.call-update) | async-done | bytes 2097168 | tf_op jit(solution)/shard_map/all_gather | solution.py:36
  250.4 61.8 %while.31 = (s32[]{:T(128)}, f32[64,32,128]{2,1,0:T(8,128)S(1)}, s32[]{:T(128)}, s32[96]{0:T(128)S(1)}, bf16[96,32,128]{2,1,0:T(8,128)(2,1)}, /*index=5*/s32[96]...) while((s32[]{:T(128)}, f32[64,32,128]{2,1,0:T(8,128)S(1)}, ...), condition=%wide.region_12.13_spmd, body=%wide.region_10.12_spmd.sunk | while | flops 83952720 | bytes 2691551 | solution.py:60
  250.5 2.2 gather_fusion.1
  256.7 2.2 gather_fusion.1
  262.8 2.2 gather_fusion.1
  269.0 2.2 gather_fusion.1
  275.2 2.2 gather_fusion.1
  281.4 2.2 gather_fusion.1
  287.6 2.2 gather_fusion.1
  293.7 2.2 gather_fusion.1
  299.9 2.2 gather_fusion.1
  306.1 2.2 gather_fusion.1
  313.3 38.7 %reduce-scatter.6.cloned.1.call-done = f32[16,32,128]{2,1,0:T(8,128)} async-done(((f32[64,32,128]{2,1,0:T(8,128)}), f32[16,32,128]{2,1,0:T(8,128)}) %reduce-scatter.6.cloned.1.call-update) | async-done | bytes 262160 | tf_op jit(solution)/shard_map/reduce_scatter | solution.py:61
  351.9 1.7 fusion.22
  355.1 31.1 %all-reduce = (f32[2]{0:T(128)S(1)}, f32[]{:T(128)}) all-reduce(f32[2]{0:T(128)S(1)} %pad_maximum_fusion.1, f32[]{:T(128)} %get-tuple-element.156), channel_id=1, replica_groups=mesh['parts'=2,'row'=4,'col'=4] {'row','col'}, use_global_device_ids=true, to_apply=%region_16.17 | all-reduce | flops 3 | bytes 24 | tf_op jit(solution)/shard_map/psum | solution.py:28
  390.4 30.1 %psum.47 = f32[]{:T(128)} all-reduce(f32[]{:T(128)} %multiply_reduce_fusion), channel_id=1, replica_groups=mesh['parts'=2,'row'=4,'col'=4] {'row','col'}, use_global_device_ids=true, to_apply=%region_20.21 | all-reduce | flops 1 | bytes 8 | tf_op jit(solution)/shard_map/psum | solution.py:28
  422.2 17.0 %all_gather.18 = bf16[64,32,128]{2,1,0:T(8,128)(2,1)} all-gather(bf16[16,32,128]{2,1,0:T(8,128)(2,1)S(1)} %multiply_convert_fusion), channel_id=1, replica_groups=mesh['parts'=2,'row'=4,'col'=4] {'row'}, dimensions={0}, use_global_device_ids=true | all-gather | bytes 655360 | tf_op jit(solution)/shard_map/all_gather | solution.py:82
  439.4 20.1 %all-gather.8.cloned.1.call-done = bf16[64,128,128]{2,1,0:T(8,128)(2,1)} async-done(((bf16[64,32,128]{2,1,0:T(8,128)(2,1)}), bf16[64,128,128]{2,1,0:T(8,128)(2,1)}) %all-gather.8.cloned.1.call-update) | async-done | bytes 2097168 | tf_op jit(solution)/shard_map/all_gather | solution.py:36
  459.6 61.8 %while.32 = (s32[]{:T(128)}, f32[64,32,128]{2,1,0:T(8,128)S(1)}, s32[]{:T(128)}, s32[96]{0:T(128)S(1)}, bf16[96,32,128]{2,1,0:T(8,128)(2,1)}, /*index=5*/s32[96]...) while((s32[]{:T(128)}, f32[64,32,128]{2,1,0:T(8,128)S(1)}, ...), condition=%wide.region_23.24_spmd, body=%wide.region_21.23_spmd.sunk | while | flops 83952720 | bytes 2691551 | solution.py:60
  459.7 2.2 gather_fusion.2
  465.9 2.2 gather_fusion.2
  472.1 2.2 gather_fusion.2
  478.2 2.2 gather_fusion.2
  484.4 2.2 gather_fusion.2
  490.6 2.2 gather_fusion.2
  496.8 2.2 gather_fusion.2
  503.0 2.2 gather_fusion.2
  509.1 2.2 gather_fusion.2
  515.3 2.2 gather_fusion.2
  522.4 38.8 %reduce-scatter.8.cloned.1.call-done = f32[16,32,128]{2,1,0:T(8,128)} async-done(((f32[64,32,128]{2,1,0:T(8,128)}), f32[16,32,128]{2,1,0:T(8,128)}) %reduce-scatter.8.cloned.1.call-update) | async-done | bytes 262160 | tf_op jit(solution)/shard_map/reduce_scatter | solution.py:61
  (219 shorter events, 139.5 us)
Async XLA Ops:
  6.5 29.1 %all-gather.4.cloned.1.call-start = ((), (), s32[]{:S(2)}) async-start(), calls=%async_computation.3 | async-start | bytes 2621440 | tf_op jit(solution)/shard_map/all_gather | solution.py:36
  10.2 135.3 %reduce-scatter.4.cloned.1.call-start = ((), (), s32[]{:S(2)}) async-start(), calls=%async_computation.4 | async-start | bytes 1310720 | tf_op jit(solution)/shard_map/reduce_scatter | solution.py:61
  35.8 109.7 %copy-start.3 = (bf16[64,32,128]{2,1,0:T(8,128)(2,1)S(1)}, bf16[64,32,128]{2,1,0:T(8,128)(2,1)}, u32[]{:S(2)}) copy-start(bf16[64,32,128]{2,1,0:T(8,128)(2,1)} %select_convert_fusion) | copy-start | bytes 1572868
  104.4 1.0 copy-start.1
  104.4 146.0 %copy-start.4 = (s32[96]{0:T(128)S(1)}, s32[96]{0:T(128)}, u32[]{:S(2)}) copy-start(s32[96]{0:T(128)} %get-tuple-element.550) | copy-start | bytes 1156
  104.4 145.9 %copy-start.5 = (s32[96]{0:T(128)S(1)}, s32[96]{0:T(128)}, u32[]{:S(2)}) copy-start(s32[96]{0:T(128)} %get-tuple-element.552) | copy-start | bytes 1156
  105.4 144.8 %all-gather.6.cloned.1.call-start = ((), (), s32[]{:S(2)}) async-start(), calls=%async_computation.5 | async-start | bytes 2621440 | tf_op jit(solution)/shard_map/all_gather | solution.py:36
  230.1 121.9 %reduce-scatter.6.cloned.1.call-start = ((), (), s32[]{:S(2)}) async-start(), calls=%async_computation.6 | async-start | bytes 1310720 | tf_op jit(solution)/shard_map/reduce_scatter | solution.py:61
  312.2 1.0 copy-start.2
  313.2 146.3 %all-gather.8.cloned.1.call-start = ((), (), s32[]{:S(2)}) async-start(), calls=%async_computation.7 | async-start | bytes 2621440 | tf_op jit(solution)/shard_map/all_gather | solution.py:36
  439.3 121.9 %reduce-scatter.8.cloned.1.call-start = ((), (), s32[]{:S(2)}) async-start(), calls=%async_computation.8 | async-start | bytes 1310720 | tf_op jit(solution)/shard_map/reduce_scatter | solution.py:61
  521.4 1.0 copy-start
Sparse Core Ops, SparseCore 0:
  10.3 25.2 all-gather.3
  105.5 39.9 reduce-scatter.3
  230.2 19.9 all-gather.5
  313.3 38.5 reduce-scatter.5
  439.4 19.9 all-gather.7
  522.5 38.5 reduce-scatter.7
where the time goes:
time: 575 us; the launch traced here: 570 us
  waiting for transfers between devices  182 us (32%)
  blocking collectives  157 us (27%)
  matrix products  71.3 us (12%)
  other arithmetic  69.6 us (12%)
  local copies, waits for them, and re-layouts  69.5 us (12%)
  between operations  18.8 us (3%)
    psum x4, blocking collectives, global_sums(): return lax.psum(values, ('row', 'col'))  122 us
    reduce_scatter x3, waiting for transfers between devices, body(): lax.psum_scatter(partial_value, 'row', scatter_dimension=0, tiled=True)  117 us
    gather x30, local copies, waits for them, and re-layouts, add_group(): blocks = column_part[sources]  65.6 us
    all_gather x3, waiting for transfers between devices, body(): column_part = lax.all_gather(vector_full, 'col', axis=1, tiled=True)  64.9 us
    dot_general x30, matrix products, add_group(): jnp.einsum('gwk,gkc->gwc', right_group.astype(jnp.float32), inner_part, p...  36.3 us
    dot_general x30, matrix products, add_group(): jnp.einsum('gkb,gbc->gkc', blocks, left_group, preferred_element_type=jnp...  35 us
    all_gather x2, blocking collectives, body(): vector_full = lax.all_gather(next_own, 'row', axis=0, tiled=True)  34.1 us
    scatter-add x30, other arithmetic, add_group(): return accum.at[targets].add(term_out * weights[:, None, None])  24.6 us
  transfers between devices with their start and end apart: 6, of which 6 were waited for; matrix products, arithmetic and copies ran while one was open for 0% of the time, Pallas kernels for 0%

commit v1 on v0

v1 whole, which is shorter than its diff:
```python
import functools

import jax
import jax.numpy as jnp
from jax import lax
from jax.experimental import pallas as pl
from jax.experimental.pallas import tpu as pltpu
from jax.sharding import PartitionSpec as P

MESH = pl.DeviceIdType.MESH
steps = 3
group = 8
full_code = 32440.0


def kernel(
    row_total, col_total,
    source_ref, prev_ref, last_ref, left_dim_ref, right_dim_ref,
    wave_ref, left_hbm, right_hbm,
    out_ref,
    left_ref, right_ref, vec, own_vec, accum, send_code, recv_code, send_sums, recv_sums,
    load_sem, sums_send, sums_recv, code_send, code_recv,
    z_send, z_recv, x_send, x_recv, near_send, near_recv, far_send, far_recv,
):
    sectors, own_cols, left_size = wave_ref.shape
    slots = left_ref.shape[0]
    per_row = sectors // row_total
    block_rows = per_row * own_cols
    peers = row_total * col_total
    row = lax.axis_index("row")
    col = lax.axis_index("col")
    flat = row * col_total + col
    x_col = (col + col_total // 2) % col_total
    near_col = col + 1 - 2 * (col % 2)
    cell_total = sectors * own_cols * col_total * left_size

    def peer(n):
        place = (flat + n) % peers
        return {"row": place // col_total, "col": place % col_total}

    loads = [
        pltpu.make_async_copy(left_hbm, left_ref, load_sem.at[0]),
        pltpu.make_async_copy(right_hbm, right_ref, load_sem.at[1]),
    ]
    for load in loads:
        load.start()

    barrier = pltpu.get_barrier_semaphore()

    @pl.loop(1, peers)
    def _(n):
        pl.semaphore_signal(barrier, inc=1, device_id=peer(n), device_id_type=MESH)

    row_ids = lax.broadcasted_iota(jnp.int32, (own_cols, left_size), 0) + col * own_cols
    lane_ids = lax.broadcasted_iota(jnp.int32, (own_cols, left_size), 1)

    def support(s):
        return (row_ids < right_dim_ref[s]) & (lane_ids < left_dim_ref[s])

    @pl.loop(0, sectors)
    def _(s):
        value = wave_ref[s].astype(jnp.float32)
        vec[col, s] = jnp.where(support(s), value, 0.0).astype(jnp.bfloat16)

    @pl.loop(0, per_row)
    def _(j):
        own_vec[0, j] = vec[col, row * per_row + j]

    accum[slots] = jnp.zeros((own_cols, left_size), jnp.float32)
    pl.semaphore_wait(barrier, peers - 1)

    def block_of(which, d):
        place = (row + row_total - d) % row_total
        return vec.at[which, pl.ds(place * per_row, per_row)]

    def move(which, d, send, recv, row_to, col_to):
        ref = block_of(which, d)
        return pltpu.make_async_remote_copy(
            src_ref=ref, dst_ref=ref, send_sem=send.at[d], recv_sem=recv.at[d],
            device_id={"row": row_to, "col": col_to}, device_id_type=MESH,
        )

    def z_move(d):
        ref = block_of(col, 0)
        return pltpu.make_async_remote_copy(
            src_ref=ref, dst_ref=ref, send_sem=z_send.at[d], recv_sem=z_recv.at[d],
            device_id={"row": (row + d) % row_total, "col": col}, device_id_type=MESH,
        )

    def x_move(d):
        return move(col, d, x_send, x_recv, row, x_col)

    def near_move(d):
        return move(col, d, near_send, near_recv, row, near_col)

    def far_move(d):
        return move(x_col, d, far_send, far_recv, row, near_col)

    def spread(first):
        x_move(0).start()
        if not first:
            @pl.loop(1, row_total)
            def _(d):
                z_move(d).start()
        near_move(0).start()

        @pl.loop(1, row_total)
        def _(d):
            if not first:
                z_move(d).wait_recv()
            x_move(d).start()
            near_move(d).start()

        @pl.loop(0, row_total)
        def _(d):
            x_move(d).wait_recv()
            far_move(d).start()

        @pl.loop(0, row_total)
        def _(d):
            near_move(d).wait()
            far_move(d).wait()
            x_move(d).wait_send()

        if not first:
            @pl.loop(1, row_total)
            def _(d):
                z_move(d).wait_send()

    def apply_terms():
        @pl.loop(0, slots // group)
        def _(g):
            outs = []
            for i in range(group):
                p = g * group + i
                block = vec[:, source_ref[p]].reshape(col_total * own_cols, left_size)
                part = jnp.dot(right_ref[p], block, preferred_element_type=jnp.float32)
                high = part.astype(jnp.bfloat16)
                low = (part - high.astype(jnp.float32)).astype(jnp.bfloat16)
                both = jnp.dot(
                    jnp.concatenate([high, low], axis=0), left_ref[p],
                    preferred_element_type=jnp.float32,
                )
                outs.append(both[:own_cols] + both[own_cols:])
            for i in range(group):
                p = g * group + i
                accum[p] = outs[i] + accum[prev_ref[p]]

    def code_move(d):
        return pltpu.make_async_remote_copy(
            src_ref=send_code.at[d], dst_ref=recv_code.at[d],
            send_sem=code_send.at[d], recv_sem=code_recv.at[d],
            device_id={"row": (row + d) % row_total, "col": col}, device_id_type=MESH,
        )

    def sums_move(n):
        return pltpu.make_async_remote_copy(
            src_ref=send_sums, dst_ref=recv_sums.at[n],
            send_sem=sums_send.at[n], recv_sem=sums_recv.at[n],
            device_id=peer(n), device_id_type=MESH,
        )

    def send_partials():
        def peak(s, top):
            return jnp.maximum(top, jnp.abs(accum[last_ref[s]]))

        top = lax.fori_loop(
            0, sectors, peak, jnp.full((own_cols, left_size), 1e-30, jnp.float32)
        )
        level = jnp.ceil(jnp.log2(jnp.max(top, axis=(0, 1), keepdims=True)))
        factor = jnp.exp2(-level) * full_code
        tail = jnp.broadcast_to(level, (16, left_size)).astype(jnp.int32).astype(jnp.int16)

        @pl.loop(1, row_total)
        def _(d):
            base = ((row + d) % row_total) * per_row
            send_code[d, pl.ds(block_rows, 16)] = tail

            @pl.loop(0, per_row)
            def _(j):
                value = jnp.round(accum[last_ref[base + j]] * factor)
                send_code[d, pl.ds(pl.multiple_of(j * own_cols, 16), own_cols)] = value.astype(
                    jnp.int32
                ).astype(jnp.int16)

            code_move(d).start()

    def add_partials(step):
        def scale_of(d):
            level = recv_code[d, pl.ds(block_rows, 16)].astype(jnp.int32).astype(jnp.float32)
            return jnp.exp2(level[0:1, :]) * (1.0 / full_code)

        @pl.loop(0, per_row)
        def _(j):
            out_ref[step, j] = accum[last_ref[row * per_row + j]]

        @pl.loop(1, row_total)
        def _(d):
            code_move(d).wait_recv()
            scale = scale_of(d)

            @pl.loop(0, per_row)
            def _(j):
                code = recv_code[d, pl.ds(pl.multiple_of(j * own_cols, 16), own_cols)]
                out_ref[step, j] += code.astype(jnp.int32).astype(jnp.float32) * scale

        @pl.loop(0, per_row)
        def _(j):
            out_ref[step, j] = jnp.where(support(row * per_row + j), out_ref[step, j], 0.0)

    def fold(value):
        return jnp.sum(value, axis=0, keepdims=True)

    spread(True)
    for load in loads:
        load.wait()
    grams = {}
    for step in range(steps):
        apply_terms()
        send_partials()
        add_partials(step)

        @pl.loop(1, row_total)
        def _(d):
            code_move(d).wait_send()

        if step + 1 == steps:
            break
        pairs = [(i, step) for i in range(step + 1)]
        count = 1 + (step + 1) + len(pairs)

        def add_sums(j, totals):
            sigma = out_ref[step, j]
            wide = [own_vec[i, j].astype(jnp.float32) for i in range(step + 1)]
            items = [sigma * sigma] + [entry * sigma for entry in wide]
            items += [wide[i] * wide[k] for i, k in pairs]
            return tuple(a + b for a, b in zip(totals, items))

        zero = jnp.zeros((own_cols, left_size), jnp.float32)
        totals = lax.fori_loop(0, per_row, add_sums, (zero,) * count)
        rows = [fold(total) for total in totals]
        rows += [jnp.zeros((8 - count, left_size), jnp.float32)]
        send_sums[...] = jnp.concatenate(rows, axis=0)

        @pl.loop(1, peers)
        def _(n):
            sums_move(n).start()

        def gather_sums(n, total):
            sums_move(n).wait()
            return total + recv_sums[n]

        total = lax.fori_loop(1, peers, gather_sums, send_sums[...])
        total = jnp.sum(total, axis=1, keepdims=True)
        values = [total[i : i + 1] for i in range(count)]
        square, correlations = values[0], values[1 : step + 2]
        for pair, value in zip(pairs, values[step + 2 :]):
            grams[pair] = value
        weights = [
            correlations[i] / (grams[(i, i)] + 1e-06) for i in range(step + 1)
        ]
        for i in range(step + 1):
            square = square - 2.0 * weights[i] * correlations[i]
            for k in range(step + 1):
                square = square + weights[i] * weights[k] * grams[(min(i, k), max(i, k))]
        mean_sq = jnp.maximum(square, 0.0) / cell_total
        factor = lax.rsqrt(mean_sq + 1e-06)

        @pl.loop(0, per_row)
        def _(j):
            remainder = out_ref[step, j]
            for i in range(step + 1):
                remainder = remainder - weights[i] * own_vec[i, j].astype(jnp.float32)
            fresh = (remainder * factor).astype(jnp.bfloat16)
            vec[col, row * per_row + j] = fresh
            if step + 2 < steps:
                own_vec[step + 1, j] = fresh

        spread(False)


def body(
    wavefunction, left_ops, right_ops, term_source, term_target, term_count, left_dims, right_dims
):
    row_total = lax.axis_size("row")
    col_total = lax.axis_size("col")
    peers = row_total * col_total
    sectors, own_cols, left_size = wavefunction.shape
    slots = left_ops.shape[0]
    per_row = sectors // row_total
    ids = jnp.arange(slots, dtype=jnp.int32)
    active = ids < term_count[0]
    same = (
        (term_target[:, None] == term_target[None, :])
        & active[None, :]
        & (ids[None, :] < ids[:, None])
    )
    prev = jnp.max(jnp.where(same, ids[None, :], -1), axis=1)
    prev = jnp.where(prev < 0, slots, prev)
    here = (jnp.arange(sectors, dtype=jnp.int32)[:, None] == term_target[None, :]) & active[None, :]
    last = jnp.max(jnp.where(here, ids[None, :], -1), axis=1)
    last = jnp.where(last < 0, slots, last)
    code_rows = per_row * own_cols + 16
    smem = pl.BlockSpec(memory_space=pltpu.SMEM)
    vmem = pl.BlockSpec(memory_space=pltpu.VMEM)
    hbm = pl.BlockSpec(memory_space=pl.ANY)
    dma = pltpu.SemaphoreType.DMA
    return pl.pallas_call(
        functools.partial(kernel, row_total, col_total),
        out_shape=jax.ShapeDtypeStruct((steps, per_row, own_cols, left_size), jnp.float32),
        in_specs=[smem] * 5 + [vmem, hbm, hbm],
        out_specs=vmem,
        scratch_shapes=[
            pltpu.VMEM(left_ops.shape, jnp.bfloat16),
            pltpu.VMEM(right_ops.shape, jnp.bfloat16),
            pltpu.VMEM((col_total, sectors, own_cols, left_size), jnp.bfloat16),
            pltpu.VMEM((2, per_row, own_cols, left_size), jnp.bfloat16),
            pltpu.VMEM((slots + 1, own_cols, left_size), jnp.float32),
            pltpu.VMEM((row_total, code_rows, left_size), jnp.int16),
            pltpu.VMEM((row_total, code_rows, left_size), jnp.int16),
            pltpu.VMEM((8, left_size), jnp.float32),
            pltpu.VMEM((peers, 8, left_size), jnp.float32),
            dma((2,)),
            dma((peers,)),
            dma((peers,)),
        ]
        + [dma((row_total,))] * 10,
        compiler_params=pltpu.CompilerParams(
            collective_id=0, has_side_effects=True, vmem_limit_bytes=40 * 1024 * 1024
        ),
        cost_estimate=pl.CostEstimate(
            flops=steps * slots * 6 * own_cols * left_size * left_size,
            bytes_accessed=8 * 1024 * 1024,
            transcendentals=0,
        ),
    )(term_source, prev, last, left_dims, right_dims, wavefunction, left_ops, right_ops)


def solution(mesh):
    placed = (
        P("parts", "col", None),
        P(("parts", "row"), None, None),
        P(("parts", "row"), "col", None),
        P(("parts", "row")),
        P(("parts", "row")),
        P(("parts", "row")),
        P("parts"),
        P("parts"),
    )
    return jax.shard_map(
        body,
        mesh=mesh,
        in_specs=placed,
        out_specs=P(None, ("parts", "row"), "col", None),
        check_vma=False,
    )
```

time: 575 us -> 136 us (0.24)
  waiting for transfers between devices: 182 us -> 0 us
  blocking collectives: 157 us -> 0 us
  Pallas kernels: 0 us -> 124 us
  matrix products: 71.3 us -> 0 us
  other arithmetic: 69.6 us -> 1.71 us
  local copies, waits for them, and re-layouts: 69.5 us -> 6.9 us
  between operations: 18.8 us -> 0.7 us
    pallas_call x0 -> x1, Pallas kernels: none -> 124 us  [body(): pl.pallas_call(functools.partial(kernel, row_total, col_total), out_shape...]
    psum x4 -> x0, blocking collectives: 122 us -> none  [global_sums(): return lax.psum(values, ('row', 'col'))]
    reduce_scatter x3 -> x0, waiting for transfers between devices: 117 us -> none  [body(): lax.psum_scatter(partial_value, 'row', scatter_dimension=0, tiled=True)]
    dot_general x60 -> x0, matrix products: 71.3 us -> none  [the longest x30 36.3 us: add_group(): jnp.einsum('gwk,gkc->gwc', right_group.astype(jnp.float32), inner_part, p...]
    gather x30 -> x0, local copies, waits for them, and re-layouts: 65.6 us -> none  [add_group(): blocks = column_part[sources]]
    all_gather x3 -> x0, waiting for transfers between devices: 64.9 us -> none  [body(): column_part = lax.all_gather(vector_full, 'col', axis=1, tiled=True)]
    all_gather x2 -> x0, blocking collectives: 34.1 us -> none  [body(): vector_full = lax.all_gather(next_own, 'row', axis=0, tiled=True)]
    scatter-add x30 -> x0, other arithmetic: 24.6 us -> none  [add_group(): return accum.at[targets].add(term_out * weights[:, None, None])]
  transfers between devices with their start and end apart: 6 -> 0, of which waited for: 6 -> 0; matrix products, arithmetic and copies ran while one was open for 0% -> 0% of each run, Pallas kernels for 0% -> 0%
where the time goes in v1:
time: 136 us; the launch traced here: 134 us
  Pallas kernels  124 us (91%)
  local copies, waits for them, and re-layouts  6.9 us (5%)
  other arithmetic  1.71 us (1%)
    pallas_call x1, Pallas kernels, body(): pl.pallas_call(functools.partial(kernel, row_total, col_total), out_shape...  124 us
    unnamed x13, local copies, waits for them, and re-layouts  6.9 us

profile of v1, /device:TPU:0, one launch (start us, length us, event | category | flops | bytes accessed | tf_op | source)
XLA Modules:
  0.0 133.8 jit_solution(17219004947215684083)
XLA Ops:
  0.7 0.8 select_reduce_fusion.1
  1.4 0.9 select_reduce_fusion
  2.4 0.0 copy-start
  2.4 1.9 %copy-done = bf16[96,128,128]{2,1,0:T(8,128)(2,1)S(1)} copy-done((bf16[96,128,128]{2,1,0:T(8,128)(2,1)S(1)}, bf16[96,128,128]{2,1,0:T(8,128)(2,1)}, u32[]{:S(2)}) %copy-start) | copy-done | bytes 3145752
  4.3 0.0 copy-start.1
  4.3 1.1 copy-done.1
  5.4 0.0 copy-start.2
  5.4 1.0 copy-done.2
  6.5 0.0 copy-start.3
  6.5 0.7 copy-done.3
  7.1 0.0 copy-start.4
  7.1 0.7 copy-done.4
  7.8 0.0 copy-start.5
  7.8 0.7 copy-done.5
  8.4 124.5 %shard_map.82 = f32[3,16,32,128]{3,2,1,0:T(8,128)S(1)} custom-call(s32[96]{0:T(128)S(1)} %copy-done.3, s32[96]{0:T(128)S(1)} %compare_select_fusion.1.prev_ref, s32[64]{0:T(128)S(1)} %compare_select_fusion.last_ref, s32[64]{0:T(128)S(1)} %copy-done.4, s32[64]{0:T(128)S(1)} %copy-done.5, bf16[64,32,128]{2,1,0:T(8,128)(2,1)S(1)} %copy-done.2, ...), custom_call_target="tpu_custom_call" | custom-call | flops 905969664 | bytes 8388608 | tf_op jit(solution)/shard_map/pallas_call | solution.py:308
  132.9 0.9 copy.11
  (3 shorter events, 0.0 us)
Async XLA Ops:
  2.4 1.9 %copy-start = (bf16[96,128,128]{2,1,0:T(8,128)(2,1)S(1)}, bf16[96,128,128]{2,1,0:T(8,128)(2,1)}, u32[]{:S(2)}) copy-start(bf16[96,128,128]{2,1,0:T(8,128)(2,1)} %left_hbm.1) | copy-start | bytes 9437188
  4.3 1.1 copy-start.1
  5.4 1.0 copy-start.2
  6.5 0.7 copy-start.3
  7.1 0.7 copy-start.4
  7.8 0.7 copy-start.5

commit v2 on v1

--- a/solution.py
+++ b/solution.py
@@ -11,6 +11,7 @@
 steps = 3
 group = 8
 full_code = 32440.0
+pieces, shared = 8, 3
 
 
 def kernel(
@@ -18,7 +19,7 @@
     source_ref, prev_ref, last_ref, left_dim_ref, right_dim_ref,
     wave_ref, left_hbm, right_hbm,
     out_ref,
-    left_ref, right_ref, vec, own_vec, accum, send_code, recv_code, send_sums, recv_sums,
+    left_ref, right_ref, vec, own_vec, accum, total_block, send_code, recv_code, send_sums, recv_sums,
     load_sem, sums_send, sums_recv, code_send, code_recv,
     z_send, z_recv, x_send, x_recv, near_send, near_recv, far_send, far_recv,
 ):
@@ -26,6 +27,8 @@
     slots = left_ref.shape[0]
     per_row = sectors // row_total
     block_rows = per_row * own_cols
+    halves = 2 if per_row % 2 == 0 else 1
+    unroll = 4 if per_row % 4 == 0 else 1
     peers = row_total * col_total
     row = lax.axis_index("row")
     col = lax.axis_index("col")
@@ -69,63 +72,169 @@
     accum[slots] = jnp.zeros((own_cols, left_size), jnp.float32)
     pl.semaphore_wait(barrier, peers - 1)
 
-    def block_of(which, d):
-        place = (row + row_total - d) % row_total
-        return vec.at[which, pl.ds(place * per_row, per_row)]
-
-    def move(which, d, send, recv, row_to, col_to):
-        ref = block_of(which, d)
+    def move(which, start, size, send, recv, row_to, col_to):
+        ref = vec.at[which, pl.ds(start, size)]
         return pltpu.make_async_remote_copy(
-            src_ref=ref, dst_ref=ref, send_sem=send.at[d], recv_sem=recv.at[d],
+            src_ref=ref, dst_ref=ref, send_sem=send, recv_sem=recv,
             device_id={"row": row_to, "col": col_to}, device_id_type=MESH,
         )
 
-    def z_move(d):
-        ref = block_of(col, 0)
-        return pltpu.make_async_remote_copy(
-            src_ref=ref, dst_ref=ref, send_sem=z_send.at[d], recv_sem=z_recv.at[d],
-            device_id={"row": (row + d) % row_total, "col": col}, device_id_type=MESH,
-        )
-
-    def x_move(d):
-        return move(col, d, x_send, x_recv, row, x_col)
-
-    def near_move(d):
-        return move(col, d, near_send, near_recv, row, near_col)
-
-    def far_move(d):
-        return move(x_col, d, far_send, far_recv, row, near_col)
-
-    def spread(first):
-        x_move(0).start()
-        if not first:
+    def mirror(r):
+        return jnp.where(row < 2, r, 3 - r)
+
+    def spread_first():
+        size = sectors // pieces
+        side = row % 2
+        alone = [side * shared + i for i in range(shared)]
+        other = [(1 - side) * shared + i for i in range(shared)]
+        common = list(range(2 * shared, pieces))
+
+        def x_move(k):
+            return move(col, k * size, size, x_send.at[k], x_recv.at[k], row, x_col)
+
+        def pair_move(k):
+            return move(
+                x_col, k * size, size, z_send.at[k], z_recv.at[k], row + 1 - 2 * side, col
+            )
+
+        def near_move():
+            return move(col, 0, sectors, near_send.at[0], near_recv.at[0], row, near_col)
+
+        def far_move(k):
+            return move(x_col, k * size, size, far_send.at[k], far_recv.at[k], row, near_col)
+
+        for k in alone + common:
+            x_move(k).start()
+        near_move().start()
+        for k in alone:
+            x_move(k).wait_recv()
+            pair_move(k).start()
+            far_move(k).start()
+        for mine, theirs in zip(common + [None] * shared, other):
+            if mine is not None:
+                x_move(mine).wait_recv()
+                far_move(mine).start()
+            pair_move(theirs).wait_recv()
+            far_move(theirs).start()
+        for k in alone + common:
+            x_move(k).wait_send()
+        for k in alone:
+            pair_move(k).wait_send()
+        near_move().wait()
+
+        @pl.loop(0, pieces)
+        def _(k):
+            far_move(k).wait()
+
+    def spread():
+        size = per_row // halves
+
+        def part(which, b, h, send, recv, k, row_to, col_to):
+            return move(
+                which, b * per_row + h * size, size, send.at[k * halves + h],
+                recv.at[b * halves + h], row_to, col_to,
+            )
+
+        def z_move(to, h):
+            return part(col, row, h, z_send, z_recv, to, to, col)
+
+        def z_arrival(b, h):
+            return part(col, b, h, z_send, z_recv, b, row, near_col)
+
+        def relay_move(h):
+            return part(col, mirror(2), h, z_send, z_recv, row_total, mirror(0), col)
+
+        def x_move(b, h):
+            return part(col, b, h, x_send, x_recv, b, row, x_col)
+
+        def near_move(b, h):
+            return part(col, b, h, near_send, near_recv, b, row, near_col)
+
+        def far_move(b, h):
+            return part(x_col, b, h, far_send, far_recv, b, row, near_col)
+
+        def start_all(b, h):
+            x_move(b, h).start()
+            near_move(b, h).start()
+
+        def arrived(b, relay=False):
+            for h in range(halves):
+                z_arrival(b, h).wait_recv()
+                if relay:
+                    @pl.when(middle)
+                    def _():
+                        relay_move(h).start()
+                start_all(b, h)
+
+        def x_arrived(b):
+            for h in range(halves):
+                x_move(b, h).wait_recv()
+                far_move(b, h).start()
+
+        for h in range(halves):
+            x_move(row, h).start()
+        if row_total == 4:
+            middle = (row == 1) | (row == 2)
+            inner = middle.astype(jnp.int32)
+            order = [mirror(1 + inner), mirror(3 - 3 * inner), mirror(2 + inner)]
+            sends = [mirror(3 - inner), mirror(2 - 2 * inner)]
+            for to in sends:
+                for h in range(halves):
+                    z_move(to, h).start()
+
+            @pl.when(jnp.logical_not(middle))
+            def _():
+                for h in range(halves):
+                    z_move(mirror(1), h).start()
+
+            for h in range(halves):
+                near_move(row, h).start()
+            arrived(order[0], True)
+            x_arrived(row)
+            arrived(order[1])
+            x_arrived(order[0])
+            arrived(order[2])
+            x_arrived(order[1])
+            x_arrived(order[2])
+            for h in range(halves):
+                for to in sends:
+                    z_move(to, h).wait_send()
+
+                @pl.when(jnp.logical_not(middle))
+                def _():
+                    z_move(mirror(1), h).wait_send()
+
+                @pl.when(middle)
+                def _():
+                    relay_move(h).wait_send()
+        else:
             @pl.loop(1, row_total)
             def _(d):
-                z_move(d).start()
-        near_move(0).start()
-
-        @pl.loop(1, row_total)
-        def _(d):
-            if not first:
-                z_move(d).wait_recv()
-            x_move(d).start()
-            near_move(d).start()
-
-        @pl.loop(0, row_total)
-        def _(d):
-            x_move(d).wait_recv()
-            far_move(d).start()
-
-        @pl.loop(0, row_total)
-        def _(d):
-            near_move(d).wait()
-            far_move(d).wait()
-            x_move(d).wait_send()
-
-        if not first:
+                for h in range(halves):
+                    z_move((row + d) % row_total, h).start()
+
+            for h in range(halves):
+                near_move(row, h).start()
+
             @pl.loop(1, row_total)
             def _(d):
-                z_move(d).wait_send()
+                arrived((row + row_total - d) % row_total)
+
+            @pl.loop(0, row_total)
+            def _(b):
+                x_arrived(b)
+
+            @pl.loop(1, row_total)
+            def _(d):
+                for h in range(halves):
+                    z_move((row + d) % row_total, h).wait_send()
+
+        @pl.loop(0, row_total)
+        def _(b):
+            for h in range(halves):
+                near_move(b, h).wait()
+                far_move(b, h).wait()
+                x_move(b, h).wait_send()
 
     def apply_terms():
         @pl.loop(0, slots // group)
@@ -146,11 +255,11 @@
                 p = g * group + i
                 accum[p] = outs[i] + accum[prev_ref[p]]
 
-    def code_move(d):
+    def code_move(o, slot, row_to):
         return pltpu.make_async_remote_copy(
-            src_ref=send_code.at[d], dst_ref=recv_code.at[d],
-            send_sem=code_send.at[d], recv_sem=code_recv.at[d],
-            device_id={"row": (row + d) % row_total, "col": col}, device_id_type=MESH,
+            src_ref=send_code.at[o], dst_ref=recv_code.at[slot],
+            send_sem=code_send.at[o], recv_sem=code_recv.at[slot],
+            device_id={"row": row_to, "col": col}, device_id_type=MESH,
         )
 
     def sums_move(n):
@@ -160,69 +269,122 @@
             device_id=peer(n), device_id_type=MESH,
         )
 
-    def send_partials():
-        def peak(s, top):
-            return jnp.maximum(top, jnp.abs(accum[last_ref[s]]))
+    def scale_of(slot):
+        level = recv_code[slot, pl.ds(block_rows, 16)].astype(jnp.int32).astype(jnp.float32)
+        return jnp.exp2(level[0:1, :]) * (1.0 / full_code)
+
+    def rows_of(j):
+        return pl.ds(pl.multiple_of(j * own_cols, 16), own_cols)
+
+    def decode(slot, j, scale):
+        return recv_code[slot, rows_of(j)].astype(jnp.int32).astype(jnp.float32) * scale
+
+    def relay(o, slot, first):
+        scale = None if first else scale_of(slot)
+
+        def gather(j, top):
+            value = accum[last_ref[o * per_row + j]]
+            if not first:
+                value = value + decode(slot, j, scale)
+            total_block[j] = value
+            return jnp.maximum(top, jnp.abs(value))
 
         top = lax.fori_loop(
-            0, sectors, peak, jnp.full((own_cols, left_size), 1e-30, jnp.float32)
+            0, per_row, gather, jnp.full((own_cols, left_size), 1e-30, jnp.float32),
+            unroll=unroll,
         )
         level = jnp.ceil(jnp.log2(jnp.max(top, axis=(0, 1), keepdims=True)))
         factor = jnp.exp2(-level) * full_code
-        tail = jnp.broadcast_to(level, (16, left_size)).astype(jnp.int32).astype(jnp.int16)
+        send_code[o, pl.ds(block_rows, 16)] = (
+            jnp.broadcast_to(level, (16, left_size)).astype(jnp.int32).astype(jnp.int16)
+        )
+
+        @pl.loop(0, per_row, unroll=unroll)
+        def _(j):
+            value = jnp.round(total_block[j] * factor)
+            send_code[o, rows_of(j)] = value.astype(jnp.int32).astype(jnp.int16)
+
+    def reduce_partials(step):
+        def send(o):
+            relay(o, 0, True)
+            code_move(o, row, o).start()
+
+        def receive(r):
+            code_move(row, r, near_row).wait_recv()
+            scale = scale_of(r)
+
+            @pl.loop(0, per_row, unroll=unroll)
+            def _(j):
+                out_ref[step, j] += decode(r, j, scale)
+
+        near_row = (row + 1) % row_total
+
+        def take_own():
+            @pl.loop(0, per_row, unroll=unroll)
+            def _(j):
+                out_ref[step, j] = accum[last_ref[row * per_row + j]]
+
+        if row_total == 4:
+            middle = (row == 1) | (row == 2)
+            end = jnp.logical_not(middle)
+
+            @pl.when(end)
+            def _():
+                relay(mirror(3), 0, True)
+                code_move(mirror(3), row_total, mirror(1)).start()
+                send(mirror(2))
+                send(mirror(1))
+
+            @pl.when(middle)
+            def _():
+                send(mirror(2))
+                send(mirror(0))
+                code_move(row, row_total, near_row).wait_recv()
+                relay(mirror(3), row_total, False)
+                code_move(mirror(3), row, mirror(3)).start()
+
+            take_own()
+
+            @pl.when(end)
+            def _():
+                receive(mirror(1))
+                receive(mirror(2))
+
+            @pl.when(middle)
+            def _():
+                receive(mirror(2))
+                receive(mirror(0))
+                receive(mirror(3))
+        else:
+            @pl.loop(1, row_total)
+            def _(d):
+                send((row + d) % row_total)
+
+            take_own()
+
+            @pl.loop(1, row_total)
+            def _(d):
+                receive((row + row_total - d) % row_total)
+
+        @pl.loop(0, per_row, unroll=unroll)
+        def _(j):
+            out_ref[step, j] = jnp.where(support(row * per_row + j), out_ref[step, j], 0.0)
 
         @pl.loop(1, row_total)
         def _(d):
-            base = ((row + d) % row_total) * per_row
-            send_code[d, pl.ds(block_rows, 16)] = tail
-
-            @pl.loop(0, per_row)
-            def _(j):
-                value = jnp.round(accum[last_ref[base + j]] * factor)
-                send_code[d, pl.ds(pl.multiple_of(j * own_cols, 16), own_cols)] = value.astype(
-                    jnp.int32
-                ).astype(jnp.int16)
-
-            code_move(d).start()
-
-    def add_partials(step):
-        def scale_of(d):
-            level = recv_code[d, pl.ds(block_rows, 16)].astype(jnp.int32).astype(jnp.float32)
-            return jnp.exp2(level[0:1, :]) * (1.0 / full_code)
-
-        @pl.loop(0, per_row)
-        def _(j):
-            out_ref[step, j] = accum[last_ref[row * per_row + j]]
-
-        @pl.loop(1, row_total)
-        def _(d):
-            code_move(d).wait_recv()
-            scale = scale_of(d)
-
-            @pl.loop(0, per_row)
-            def _(j):
-                code = recv_code[d, pl.ds(pl.multiple_of(j * own_cols, 16), own_cols)]
-                out_ref[step, j] += code.astype(jnp.int32).astype(jnp.float32) * scale
-
-        @pl.loop(0, per_row)
-        def _(j):
-            out_ref[step, j] = jnp.where(support(row * per_row + j), out_ref[step, j], 0.0)
+            o = (row + d) % row_total
+            code_move(o, row, near_row).wait_send()
 
     def fold(value):
         return jnp.sum(value, axis=0, keepdims=True)
 
-    spread(True)
+    spread_first()
     for load in loads:
         load.wait()
     grams = {}
     for step in range(steps):
         apply_terms()
-        send_partials()
-        add_partials(step)
-
-        @pl.loop(1, row_total)
-        def _(d):
-            code_move(d).wait_send()
+        reduce_partials(step)
 
         if step + 1 == steps:
             break
@@ -237,7 +399,7 @@
             return tuple(a + b for a, b in zip(totals, items))
 
         zero = jnp.zeros((own_cols, left_size), jnp.float32)
-        totals = lax.fori_loop(0, per_row, add_sums, (zero,) * count)
+        totals = lax.fori_loop(0, per_row, add_sums, (zero,) * count, unroll=unroll)
         rows = [fold(total) for total in totals]
         rows += [jnp.zeros((8 - count, left_size), jnp.float32)]
         send_sums[...] = jnp.concatenate(rows, axis=0)
@@ -276,7 +438,7 @@
             if step + 2 < steps:
                 own_vec[step + 1, j] = fresh
 
-        spread(False)
+        spread()
 
 
 def body(
@@ -316,17 +478,19 @@
             pltpu.VMEM((col_total, sectors, own_cols, left_size), jnp.bfloat16),
             pltpu.VMEM((2, per_row, own_cols, left_size), jnp.bfloat16),
             pltpu.VMEM((slots + 1, own_cols, left_size), jnp.float32),
+            pltpu.VMEM((per_row, own_cols, left_size), jnp.float32),
             pltpu.VMEM((row_total, code_rows, left_size), jnp.int16),
-            pltpu.VMEM((row_total, code_rows, left_size), jnp.int16),
+            pltpu.VMEM((row_total + 1, code_rows, left_size), jnp.int16),
             pltpu.VMEM((8, left_size), jnp.float32),
             pltpu.VMEM((peers, 8, left_size), jnp.float32),
             dma((2,)),
             dma((peers,)),
             dma((peers,)),
         ]
-        + [dma((row_total,))] * 10,
+        + [dma((row_total + 1,))] * 2
+        + [dma((max(pieces, 2 * row_total + 2),))] * 8,
         compiler_params=pltpu.CompilerParams(
-            collective_id=0, has_side_effects=True, vmem_limit_bytes=40 * 1024 * 1024
+            collective_id=0, has_side_effects=True, vmem_limit_bytes=58 * 1024 * 1024
         ),
         cost_estimate=pl.CostEstimate(
             flops=steps * slots * 6 * own_cols * left_size * left_size,

time: 136 us -> 125 us (0.919); the launches traced: 134 us -> 125 us
  Pallas kernels: 124 us -> 119 us
  local copies, waits for them, and re-layouts: 6.9 us -> 2.06 us
    pallas_call x1, Pallas kernels: 124 us -> 119 us  [body(): pl.pallas_call(functools.partial(kernel, row_total, col_total), out_shape...]
    unnamed x13 -> x1, local copies, waits for them, and re-layouts: 6.9 us -> 2.06 us
where the time goes in v2:
time: 125 us
  Pallas kernels  119 us (95%)
  other arithmetic  2.8 us (2%)
  local copies, waits for them, and re-layouts  2.06 us (2%)
    pallas_call x1, Pallas kernels, body(): pl.pallas_call(functools.partial(kernel, row_total, col_total), out_shape...  119 us

profile of v2, /device:TPU:0, one launch (start us, length us, event | category | flops | bytes accessed | tf_op | source)
XLA Modules:
  0.0 124.7 jit_solution(12752465731165570106)
XLA Ops:
  0.7 0.8 select_reduce_fusion.1
  1.4 0.9 select_reduce_fusion
  2.4 0.5 compare_select_fusion.1.prev_ref
  2.9 0.6 compare_select_fusion.last_ref
  3.5 119.1 %shard_map.82 = f32[3,16,32,128]{3,2,1,0:T(8,128)} custom-call(s32[96]{0:T(128)} %source_ref.1, s32[96]{0:T(128)} %compare_select_fusion.1.prev_ref, s32[64]{0:T(128)} %compare_select_fusion.last_ref, s32[64]{0:T(128)} %left_dim_ref.1, s32[64]{0:T(128)} %right_dim_ref.1, bf16[64,32,128]{2,1,0:T(8,128)(2,1)} %wave_ref.1, bf16[96,128,128]{2,1,0:T(8,128)(2,1)} %left_hbm.1, ...), custom_call_target="tpu_custom_call" | custom-call | flops 905969664 | bytes 8388608 | tf_op jit(solution)/shard_map/pallas_call | solution.py:470
  122.6 2.1 %copy.11 = f32[3,16,32,128]{3,2,1,0:T(8,128)} copy(f32[3,16,32,128]{3,2,1,0:T(8,128)} %shard_map.82) | data formatting | bytes 1572864
  (1 shorter events, 0.0 us)

commit v3 on v2

--- a/solution.py
+++ b/solution.py
@@ -9,7 +9,7 @@
 
 MESH = pl.DeviceIdType.MESH
 steps = 3
-group = 8
+group = 32
 full_code = 32440.0
 pieces, shared = 8, 3
 
@@ -30,6 +30,7 @@
     halves = 2 if per_row % 2 == 0 else 1
     unroll = 4 if per_row % 4 == 0 else 1
     peers = row_total * col_total
+    peer_unroll = 15 if (peers - 1) % 15 == 0 and peers <= 32 else 1
     row = lax.axis_index("row")
     col = lax.axis_index("col")
     flat = row * col_total + col
@@ -60,7 +61,7 @@
     def support(s):
         return (row_ids < right_dim_ref[s]) & (lane_ids < left_dim_ref[s])
 
-    @pl.loop(0, sectors)
+    @pl.loop(0, sectors, unroll=4)
     def _(s):
         value = wave_ref[s].astype(jnp.float32)
         vec[col, s] = jnp.where(support(s), value, 0.0).astype(jnp.bfloat16)
@@ -404,7 +405,7 @@
         rows += [jnp.zeros((8 - count, left_size), jnp.float32)]
         send_sums[...] = jnp.concatenate(rows, axis=0)
 
-        @pl.loop(1, peers)
+        @pl.loop(1, peers, unroll=peer_unroll)
         def _(n):
             sums_move(n).start()
 
@@ -412,7 +413,7 @@
             sums_move(n).wait()
             return total + recv_sums[n]
 
-        total = lax.fori_loop(1, peers, gather_sums, send_sums[...])
+        total = lax.fori_loop(1, peers, gather_sums, send_sums[...], unroll=peer_unroll)
         total = jnp.sum(total, axis=1, keepdims=True)
         values = [total[i : i + 1] for i in range(count)]
         square, correlations = values[0], values[1 : step + 2]

time: 125 us -> 118 us (0.944)
  Pallas kernels: 119 us -> 112 us
    pallas_call x1, Pallas kernels: 119 us -> 112 us  [body(): pl.pallas_call(functools.partial(kernel, row_total, col_total), out_shape...]
where the time goes in v3:
time: 118 us
  Pallas kernels  112 us (95%)
  other arithmetic  2.8 us (2%)
  local copies, waits for them, and re-layouts  2.06 us (2%)
    pallas_call x1, Pallas kernels, body(): pl.pallas_call(functools.partial(kernel, row_total, col_total), out_shape...  112 us

profile of v3, /device:TPU:0, one launch (start us, length us, event | category | flops | bytes accessed | tf_op | source)
XLA Modules:
  0.0 117.9 jit_solution(5301731248799979391)
XLA Ops:
  0.7 0.8 select_reduce_fusion.1
  1.4 0.9 select_reduce_fusion
  2.4 0.5 compare_select_fusion.1.prev_ref
  2.9 0.6 compare_select_fusion.last_ref
  3.5 112.4 %shard_map.82 = f32[3,16,32,128]{3,2,1,0:T(8,128)} custom-call(s32[96]{0:T(128)} %source_ref.1, s32[96]{0:T(128)} %compare_select_fusion.1.prev_ref, s32[64]{0:T(128)} %compare_select_fusion.last_ref, s32[64]{0:T(128)} %left_dim_ref.1, s32[64]{0:T(128)} %right_dim_ref.1, bf16[64,32,128]{2,1,0:T(8,128)(2,1)} %wave_ref.1, bf16[96,128,128]{2,1,0:T(8,128)(2,1)} %left_hbm.1, ...), custom_call_target="tpu_custom_call" | custom-call | flops 905969664 | bytes 8388608 | tf_op jit(solution)/shard_map/pallas_call | solution.py:471
  115.8 2.1 %copy.11 = f32[3,16,32,128]{3,2,1,0:T(8,128)} copy(f32[3,16,32,128]{3,2,1,0:T(8,128)} %shard_map.82) | data formatting | bytes 1572864
  (1 shorter events, 0.0 us)

commit v4 on v3

--- a/solution.py
+++ b/solution.py
@@ -9,7 +9,7 @@
 
 MESH = pl.DeviceIdType.MESH
 steps = 3
-group = 32
+group = 48
 full_code = 32440.0
 pieces, shared = 8, 3
 
@@ -230,7 +230,7 @@
                 for h in range(halves):
                     z_move((row + d) % row_total, h).wait_send()
 
-        @pl.loop(0, row_total)
+        @pl.loop(0, row_total, unroll=unroll)
         def _(b):
             for h in range(halves):
                 near_move(b, h).wait()

time: 118 us -> 117 us (level)
  no operation moved by 1% of the time
where the time goes in v4:
time: 117 us
  Pallas kernels  112 us (96%)
  other arithmetic  2.8 us (2%)
  local copies, waits for them, and re-layouts  2.06 us (2%)
    pallas_call x1, Pallas kernels, body(): pl.pallas_call(functools.partial(kernel, row_total, col_total), out_shape...  112 us

profile of v4, /device:TPU:0, one launch (start us, length us, event | category | flops | bytes accessed | tf_op | source)
XLA Modules:
  0.0 117.2 jit_solution(13053100492000932834)
XLA Ops:
  0.7 0.8 select_reduce_fusion.1
  1.4 0.9 select_reduce_fusion
  2.4 0.5 compare_select_fusion.1.prev_ref
  2.9 0.6 compare_select_fusion.last_ref
  3.5 111.6 %shard_map.82 = f32[3,16,32,128]{3,2,1,0:T(8,128)} custom-call(s32[96]{0:T(128)} %source_ref.1, s32[96]{0:T(128)} %compare_select_fusion.1.prev_ref, s32[64]{0:T(128)} %compare_select_fusion.last_ref, s32[64]{0:T(128)} %left_dim_ref.1, s32[64]{0:T(128)} %right_dim_ref.1, bf16[64,32,128]{2,1,0:T(8,128)(2,1)} %wave_ref.1, bf16[96,128,128]{2,1,0:T(8,128)(2,1)} %left_hbm.1, ...), custom_call_target="tpu_custom_call" | custom-call | flops 905969664 | bytes 8388608 | tf_op jit(solution)/shard_map/pallas_call | solution.py:471
  115.1 2.1 %copy.11 = f32[3,16,32,128]{3,2,1,0:T(8,128)} copy(f32[3,16,32,128]{3,2,1,0:T(8,128)} %shard_map.82) | data formatting | bytes 1572864
  (1 shorter events, 0.0 us)
